TPU v7x, 256 devices: a whole 4x4x8 slice. The times are simulated.
256 devices in a mesh: occ: 8 (over z_hi, core), vir: 32 (over z_lo, y, x).
Axes of the slice: x: 4, y: 4, z: 8 (z_hi: 4, z_lo: 2; z = z_hi * 2 + z_lo), core: 2. Of those that a mesh axis runs over, the one named last changes fastest.
Arguments:
- amplitudes: bfloat16 [2256, 12288], P('occ', 'vir'), may hold values from -6 to 6
- ladder_ints: bfloat16 [12288, 12288], P('vir', 'occ'), as said below
- tile_map: int32 [96, 96], replicated, may hold values from 0 to 1, as said below
- hole_ints: bfloat16 [2256, 2256], P('occ'), may hold values from -0.125 to 0.125
- occ_energy: float32 [48], replicated, may hold values from -2 to -0.3
- pair_list: int32 [2256, 2], P('occ'), may hold values from 0 to 47, as said below
- mirror_row: int32 [2256], P('occ'), may hold values from 0 to 2255, as said below
Outputs:
- residual: float32 [2256, 12288], P('occ', 'vir')
Inputs may be any that keep to these rules, and one draw needn't show every extreme that they name: symmetric: ladder_ints[ab, cd] equals ladder_ints[cd, ab]. `tile_map`: symmetric. `pair_list`: each ordered pair of distinct orbitals of the 48 occupied ones stands in exactly one row. Row mirror_row[r] holds the pair of row r reversed.
All inputs are finite; a program needn't handle non-finite values.
Results may differ from a plain program's by a relative error of at most 0.0003.
Values may be sent and summed in bfloat16 or wider, within the bound.
A program may use at most 64 MiB of HBM per device.

v0:
```python
import jax
import jax.numpy as jnp
from jax import lax
from jax.experimental import pallas as pl
from jax.experimental.pallas import tpu as pltpu
from jax.sharding import PartitionSpec as P

TILE = 128
OCC = 8
ROWS = 282
PAD = 288
HALF = 144
UP = 128
DOWN = PAD - UP
COLS = 384
ALL = OCC * PAD
MESH = pl.DeviceIdType.MESH
F32 = jnp.float32
BF16 = jnp.bfloat16


def place():
    occ = lax.axis_index("occ")
    vir = lax.axis_index("vir")
    return vir % 4, (vir // 4) % 4, (occ // 2) * 2 + vir // 16, occ % 2


def device(x, y, z, c):
    x, y, z, c = (x + 4) % 4, (y + 4) % 4, (z + 8) % 8, c % 2
    return ((z // 2) * 2 + c, (z % 2) * 16 + y * 4 + x)


def swap_pairs(m):
    lane = lax.broadcasted_iota(jnp.int32, m.shape, 1)
    return jnp.where(lane % 2 == 0, pltpu.roll(m, COLS - 1, 1), pltpu.roll(m, 1, 1))


def encode(s, rows):
    row = lax.broadcasted_iota(jnp.int32, s.shape, 0)
    s = jnp.where(row < rows, s, 0.0)
    most = jnp.max(jnp.abs(s), axis=0, keepdims=True)
    power = jnp.floor(jnp.log2(jnp.maximum(most, 1e-30)) + 1.001)
    scaled = jnp.clip(jnp.round(s * jnp.exp2(15.0 - power)), -32767.0, 32767.0)
    return jnp.where(row < rows, scaled, power).astype(jnp.int32).astype(jnp.int16)


def decode(q, rows):
    wide = q.astype(jnp.int32).astype(F32)
    row = lax.broadcasted_iota(jnp.int32, wide.shape, 0)
    return jnp.where(row < rows, wide * jnp.exp2(wide[rows : rows + 1, :] - 15.0), 0.0)


def up_rows(s):
    return encode(jnp.concatenate([s, jnp.zeros((16, COLS), F32)], axis=0), UP)


def down_rows(s):
    return encode(s, ROWS - UP)


def kernel(
    t_ref, v_ref, tiles_ref, w_ref, energy_ref, pair_ref, mirror_ref, out_ref,
    v_buf, w_buf, tiles_buf, in_sem, tpad, wp, mirror_own, turn, tall, tp, vm, ladder, split, perm, mirrors, to_core, from_core,
    up_out, up_in, down_out, down_in, keep_up, keep_down,
    s1_send, s1_recv, mr_send, mr_recv, sw_send, st_send, st_recv, tz_send, tz_recv,
    tc_send, tc_recv, pc_send, pc_recv, up_send, up_recv, down_send, down_recv,
):
    x, y, z, c = place()
    h, zlo = z // 2, z % 2
    q = 2 * h + c
    vir = zlo * 16 + y * 4 + x

    to_first = device(
        x, y + h, 4 * zlo + 2 * (y // 2) + (1 + c + y) % 2, y % 2
    )
    from_y = q % 4
    blk_direct = (1 + zlo + c) % 2
    from_first = device(x, from_y, 2 * ((y - from_y + 4) % 4) + q // 4, blk_direct)
    partner = device(x, y, z + 1 - 2 * zlo, c)
    other = device(x, y, z, c + 1)

    load_v = pltpu.make_async_copy(v_ref, v_buf, in_sem.at[0])
    load_v.start()
    load_tiles = pltpu.make_async_copy(tiles_ref, tiles_buf, in_sem.at[1])
    load_tiles.start()
    load_w = pltpu.make_async_copy(w_ref, w_buf, in_sem.at[2])
    load_w.start()
    barrier = pltpu.get_barrier_semaphore()
    peers = [
        to_first, from_first, partner, other,
        device(x + 1, y, z, c), device(x - 1, y, z, c),
        device(x, y + 1, z, c), device(x, y - 1, z, c),
    ]
    for dz in (2, 4, 6):
        for dc in (0, 1):
            peers.append(device(x, y, z + dz, c + dc))
    for peer in peers:
        pl.semaphore_signal(barrier, 1, device_id=peer, device_id_type=MESH)
    tpad[PAD - 16 :, :] = jnp.zeros((16, COLS), BF16)
    tpad[:ROWS, :] = t_ref[...]
    row = mirror_ref[...]
    for i in range(1, OCC):
        row += jnp.where(mirror_ref[...] >= i * ROWS, PAD - ROWS, 0)
    mirror_own[...] = jnp.full((8, COLS), -1.0, F32)
    mirror_own[0:1, :ROWS] = row.astype(F32)
    pl.semaphore_wait(barrier, len(peers))

    def slot(s, f, g):
        half, blk = s % 2, (blk_direct + s // 2) % 2
        xx = (x + f * (1 - half) + g * half + 8) % 4
        yy = (y + f * half + g * (1 - half) + 8) % 4
        return xx, yy, blk, half, (yy * 4 + xx) * 4 + blk * 2 + half

    def remote(src, dst, send, recv, dev):
        return pltpu.make_async_remote_copy(
            src_ref=src, dst_ref=dst, send_sem=send, recv_sem=recv, device_id=dev, device_id_type=MESH
        )

    first = []
    their_slot = (((y + h) % 4) * 4 + x) * 4 + c * 2
    for half in range(2):
        copy = remote(
            tpad.at[pl.ds(half * HALF, HALF)], tall.at[their_slot + half],
            s1_send.at[half], s1_recv.at[half], to_first,
        )
        copy.start()
        first.append(copy)

    mirror_copies = []
    n = 0
    for dz in (0, 2, 4, 6):
        for dc in (0, 1):
            if dz == 0 and dc == 0:
                continue
            copy = remote(
                mirror_own, mirrors.at[q], mr_send.at[n], mr_recv.at[n],
                device(x, y, z + dz, c + dc),
            )
            copy.start()
            mirror_copies.append(copy)
            n += 1
    mirrors[q] = mirror_own[...]
    core_own = remote(tpad, tp.at[q], tc_send.at[0], tc_recv.at[0], other)
    core_own.start()
    tp[q] = tpad[...]

    load_v.wait()
    load_tiles.wait()
    for i in range(COLS // TILE):
        for j in range(12):
            keep = tiles_buf[vir * 3 + i, q * 12 + j].astype(F32)
            part = v_buf[i * TILE : (i + 1) * TILE, j * TILE : (j + 1) * TILE].astype(F32)
            vm[j // 3, (j % 3) * TILE : (j % 3 + 1) * TILE, i * TILE : (i + 1) * TILE] = (
                (part * keep).T.astype(BF16)
            )
    ladder[...] = jnp.zeros_like(ladder)

    def step(s, ev, f, g, second, dirn):
        half = s % 2
        along_x = (1 - half) if second == 0 else half
        dev = device(x + dirn * along_x, y + dirn * (1 - along_x), z, c)
        ref = tall.at[slot(s, f, g)[4]]
        return remote(ref, ref, st_send.at[s, ev], st_recv.at[s, ev], dev)

    def spread(s, f):
        step(s, 4 + 3 * f, f, 0, 1, 1).start()
        step(s, 5 + 3 * f, f, 0, 1, -1).start()

    def begin(s):
        step(s, 1, 0, 0, 0, 1).start()
        step(s, 2, 0, 0, 0, -1).start()
        spread(s, 0)

    def rows_of(yy, blk, half):
        at = (2 * ((yy - from_y + 4) % 4) + blk) * PAD + half * HALF
        return pl.ds(pl.multiple_of(at, 16), HALF)

    def add(half, f, g):
        xx, yy = slot(half, f, g)[:2]
        at = (yy * 4 + xx) * 4 + half
        both = jnp.concatenate([tall[at], tall[at + 2]], axis=0)
        product = jnp.dot(both, vm[xx], preferred_element_type=F32)
        ladder[rows_of(yy, 0, half), :] += product[:HALF]
        ladder[rows_of(yy, 1, half), :] += product[HALF:]

    def first_side(s):
        step(s, 1, -1, 0, 0, 1).wait_recv()
        if s < 2:
            step(s, 3, -1, 0, 0, 1).start()
        spread(s, 3)
        step(s, 2, 1, 0, 0, 1).wait_recv()
        if s >= 2:
            step(s, 3, 1, 0, 0, -1).start()
        spread(s, 1)

    swaps = []
    for s in range(2):
        first[s].wait_recv()
        ref = tall.at[slot(s, 0, 0)[4]]
        copy = remote(ref, ref, sw_send.at[s], st_recv.at[2 + s, 0], partner)
        copy.start()
        swaps.append(copy)
        begin(s)
    far = []
    for i, dz in enumerate((4, 2, 6)):
        copy = remote(tpad, tp.at[q], tz_send.at[i], tz_recv.at[i], device(x, y, z + dz, c))
        copy.start()
        far.append(copy)
    for s in range(2):
        first_side(s)
    for s in range(2, 4):
        ref = tall.at[slot(s, 0, 0)[4]]
        remote(ref, ref, sw_send.at[s - 2], st_recv.at[s, 0], partner).wait_recv()
        begin(s)
    for s in range(2, 4):
        first_side(s)

    for copy in mirror_copies:
        copy.wait_recv()
    energy = jnp.zeros((2, ROWS), F32)
    for i in range(energy_ref.shape[0]):
        energy += jnp.where(pair_ref[...] == i, energy_ref[i], 0.0)
    turn[...] = jnp.zeros_like(turn)
    for i in range(OCC):
        turn[i : i + 1, :] = mirrors[i][0:1, :]
    turn[OCC : OCC + 1, :ROWS] = energy[0:1] + energy[1:2]
    columns = turn[...].T
    for i in range(OCC):
        there = lax.broadcasted_iota(jnp.int32, (PAD, ALL), 1).astype(F32)
        perm[i * PAD : (i + 1) * PAD, :] = (columns[:PAD, i : i + 1] == there).astype(BF16)

    for s in range(4):
        step(s, 3, 2, 0, 0, 1).wait_recv()
        spread(s, 2)

    def along_first(j, _):
        add(j % 2, j // 2, 0)
        return _

    lax.fori_loop(0, 8, along_first, 0)

    load_w.wait()
    wp[...] = jnp.zeros_like(wp)
    for i in range(OCC):
        wp[i, :ROWS, :ROWS] = w_buf[:, i * ROWS : (i + 1) * ROWS]

    def later(k):
        return (3 * k + (k // 2) * (3 - 2 * (k % 2))) % 4

    def along_second(j, _):
        half, f = j % 2, later(j // 2)
        for s in (half, half + 2):
            step(s, 4 + 3 * f, f, -1, 1, 1).wait_recv()
            step(s, 5 + 3 * f, f, 1, 1, 1).wait_recv()
            dirn = 1 - 2 * ((f + s // 2) % 2)
            step(s, 6 + 3 * f, f, -dirn, 1, dirn).start()
        add(half, f, -1)
        add(half, f, 1)
        return _

    lax.fori_loop(0, 4, along_second, 0)
    core_far = []
    for i, dz in enumerate((4, 2, 6)):
        far[i].wait_recv()
        theirs = ((h - dz // 2 + 4) % 4) * 2 + c
        copy = remote(tp.at[theirs], tp.at[theirs], tc_send.at[1 + i], tc_recv.at[1 + i], other)
        copy.start()
        core_far.append(copy)
    lax.fori_loop(4, 8, along_second, 0)

    core_own.wait_recv()
    for copy in core_far:
        copy.wait_recv()
    hole = jnp.zeros((PAD, COLS), F32)
    for i in range(OCC):
        hole += jnp.dot(wp[i], tp[i, :, :], preferred_element_type=F32)
    mine = pl.multiple_of(q * PAD, 16)
    ladder[pl.ds(mine, PAD), :] += hole
    ladder[pl.ds(mine, ROWS), :] -= columns[:ROWS, OCC : OCC + 1] * t_ref[...].astype(F32)

    def split_rows(s, f, g):
        xx, yy, blk, half, slot_at = slot(s, f, g)
        at = rows_of(yy, blk, half)
        m = swap_pairs(ladder[at, :])
        upper = m.astype(BF16)
        split[at, :COLS] = upper
        split[at, COLS:] = (m - upper.astype(F32)).astype(BF16)

    def split_first(j, _):
        g = j // 2
        split_rows(2 * (j % 2), 0, g + g // 2)
        return _

    lax.fori_loop(0, 6, split_first, 0)

    def across_second(j, _):
        f = later(j)
        for half in range(2):
            for s in (half, half + 2):
                step(s, 6 + 3 * f, f, 2, 1, 1).wait_recv()
            add(half, f, 2)
        split_rows(1, f, 0)
        split_rows(3, f, 0)
        return _

    lax.fori_loop(0, 4, across_second, 0)
    for s in (0, 2):
        split_rows(s, 0, 2)

    def symmetric(d):
        at = pl.ds(pl.multiple_of(d * PAD, 16), PAD)
        m = jnp.dot(perm[at, :], split[...], preferred_element_type=F32)
        return ladder[at, :] + m[:, :COLS] + m[:, COLS:]

    core_sums = []

    def core_sum(i, dh):
        to_core[i] = symmetric(((h + dh) % 4) * 2 + 1 - c)
        copy = remote(to_core.at[i], from_core.at[i], pc_send.at[i], pc_recv.at[i], other)
        copy.start()
        core_sums.append(copy)
        total = symmetric(((h + dh) % 4) * 2 + c)
        copy.wait_recv()
        return total + from_core[i]

    ahead, behind = device(x, y, z + 2, c), device(x, y, z - 2, c)

    def go(out, into, sends, recvs, i, dev):
        copy = remote(out.at[i], into.at[i], sends.at[i], recvs.at[i], dev)
        copy.start()
        return copy

    total = core_sum(0, 2)
    up_out[0] = up_rows(total[:UP])
    up_far = go(up_out, up_in, up_send, up_recv, 0, ahead)
    down_out[0] = down_rows(total[UP:])
    down_far = go(down_out, down_in, down_send, down_recv, 0, behind)
    total = core_sum(1, 1)
    down_out[1] = down_rows(total[UP:])
    down_ahead = go(down_out, down_in, down_send, down_recv, 1, ahead)
    keep_up[...] = total[:UP]
    total = core_sum(2, 3)
    up_out[1] = up_rows(total[:UP])
    up_behind = go(up_out, up_in, up_send, up_recv, 1, behind)
    keep_down[...] = total[UP:]
    up_far.wait_recv()
    up_out[2] = up_rows(keep_up[...] + decode(up_in[0], UP)[:UP])
    up_ahead = go(up_out, up_in, up_send, up_recv, 2, ahead)
    down_far.wait_recv()
    down_out[2] = down_rows(keep_down[...] + decode(down_in[0], ROWS - UP))
    down_behind = go(down_out, down_in, down_send, down_recv, 2, behind)
    total = core_sum(3, 0)
    down_ahead.wait_recv()
    up_behind.wait_recv()
    upper = total[:UP] + decode(up_in[1], UP)[:UP]
    lower = total[UP:] + decode(down_in[1], ROWS - UP)
    up_ahead.wait_recv()
    out_ref[:UP, :] = upper + decode(up_in[2], UP)[:UP]
    down_behind.wait_recv()
    out_ref[UP:, :] = lower + decode(down_in[2], ROWS - UP)
    sums = [up_far, down_far, down_ahead, up_behind, up_ahead, down_behind]

    for copy in first + mirror_copies + [core_own] + swaps + far + core_far + core_sums + sums:
        copy.wait_send()

    def sent(j, _):
        step(j % 4, 1 + j // 4, 0, 0, 0, 1).wait_send()
        return _

    lax.fori_loop(0, 60, sent, 0)


def shards(amplitudes, ladder_ints, tile_map, hole_ints, occ_energy, pair_list, mirror_row):
    vmem = pl.BlockSpec(memory_space=pltpu.VMEM)
    smem = pl.BlockSpec(memory_space=pltpu.SMEM)
    hbm = pl.BlockSpec(memory_space=pl.ANY)
    dma = pltpu.SemaphoreType.DMA
    out = pl.pallas_call(
        kernel,
        name="ladder",
        out_shape=jax.ShapeDtypeStruct((PAD, COLS), F32),
        in_specs=[vmem, hbm, hbm, hbm, smem, vmem, vmem],
        out_specs=vmem,
        scratch_shapes=[
            pltpu.VMEM(ladder_ints.shape, BF16),
            pltpu.VMEM(hole_ints.shape, BF16),
            pltpu.SMEM(tile_map.shape, jnp.int32),
            dma((3,)),
            pltpu.VMEM((PAD, COLS), BF16),
            pltpu.VMEM((OCC, PAD, PAD), BF16),
            pltpu.VMEM((8, COLS), F32),
            pltpu.VMEM((TILE, COLS), F32),
            pltpu.VMEM((64, HALF, COLS), BF16),
            pltpu.VMEM((OCC, PAD, COLS), BF16),
            pltpu.VMEM((4, COLS, COLS), BF16),
            pltpu.VMEM((ALL, COLS), F32),
            pltpu.VMEM((ALL, 2 * COLS), BF16),
            pltpu.VMEM((ALL, ALL), BF16),
            pltpu.VMEM((OCC, 8, COLS), F32),
            pltpu.VMEM((4, PAD, COLS), F32),
            pltpu.VMEM((4, PAD, COLS), F32),
            pltpu.VMEM((3, UP + 16, COLS), jnp.int16),
            pltpu.VMEM((3, UP + 16, COLS), jnp.int16),
            pltpu.VMEM((3, DOWN, COLS), jnp.int16),
            pltpu.VMEM((3, DOWN, COLS), jnp.int16),
            pltpu.VMEM((UP, COLS), F32),
            pltpu.VMEM((DOWN, COLS), F32),
            dma((2,)), dma((2,)), dma((7,)), dma((7,)), dma((2,)), dma((4, 16)), dma((4, 16)),
            dma((3,)), dma((3,)), dma((4,)), dma((4,)), dma((4,)), dma((4,)), dma((3,)), dma((3,)),
            dma((3,)), dma((3,)),
        ],
        compiler_params=pltpu.CompilerParams(
            collective_id=0, has_side_effects=True, vmem_limit_bytes=56 << 20
        ),
        cost_estimate=pl.CostEstimate(
            flops=2 * ALL * COLS * (1536 + 2 * ALL), bytes_accessed=6 << 20, transcendentals=0
        ),
    )(
        amplitudes, ladder_ints, tile_map, hole_ints, occ_energy, pair_list.T,
        mirror_row.reshape(1, -1),
    )
    return out[:ROWS]


def solution(mesh):
    return jax.shard_map(
        shards,
        mesh=mesh,
        in_specs=(
            P("occ", "vir"),
            P("vir", "occ"),
            P(),
            P("occ", None),
            P(),
            P("occ", None),
            P("occ"),
        ),
        out_specs=P("occ", "vir"),
        check_vma=False,
    )
```

profile of v0, /device:TPU:11, one launch (start us, length us, event | category | flops | bytes accessed | tf_op | source)
XLA Modules:
  0.0 90.5 jit_solution(6508252408115117134)
XLA Ops:
  0.0 1.2 %reshape.3.mirror_ref = s32[1,282]{1,0:T(1,128)} reshape(s32[282]{0:T(512)} %param.13) | data formatting | bytes 2256 | tf_op jit(solution)/shard_map/reshape | solution.py:420
  1.2 87.4 %ladder.1 = f32[288,384]{1,0:T(8,128)} custom-call(bf16[282,384]{1,0:T(8,128)(2,1)} %t_ref.1, bf16[384,1536]{1,0:T(8,128)(2,1)} %v_ref.1, s32[96,96]{1,0:T(8,128)} %tiles_ref.1, bf16[282,2256]{1,0:T(8,128)(2,1)} %w_ref.1, f32[48]{0:T(128)} %energy_ref.1, s32[2,282]{1,0:T(2,128)} %bitcast.3, s32[1,282]{1,0:T(1,128)} %reshape.3.mirror_ref), custom_call_target="tpu_custom_call" | custom-call | flops 10871635968 | bytes 6291456 | tf_op jit(solution)/shard_map/ladder/pallas_call | solution.py:378
  88.7 1.8 %copy.9 = f32[282,384]{1,0:T(8,128)} copy(f32[282,384]{1,0:T(8,128)} %bitcast.2) | data formatting | bytes 866304
where the time goes:
time: 90.7 us; the launch traced here: 90.5 us
  Pallas kernels  87.4 us (96%)
  local copies, waits for them, and re-layouts  3.05 us (3%)
    pallas_call x1, Pallas kernels, shards(): pl.pallas_call(kernel, name='ladder', out_shape=jax.ShapeDtypeStruct((PAD...  87.4 us

commit v1 on v0

--- a/solution.py
+++ b/solution.py
@@ -98,9 +98,10 @@
         pl.semaphore_signal(barrier, 1, device_id=peer, device_id_type=MESH)
     tpad[PAD - 16 :, :] = jnp.zeros((16, COLS), BF16)
     tpad[:ROWS, :] = t_ref[...]
-    row = mirror_ref[...]
+    flat = mirror_ref[...].reshape(1, ROWS)
+    row = flat
     for i in range(1, OCC):
-        row += jnp.where(mirror_ref[...] >= i * ROWS, PAD - ROWS, 0)
+        row += jnp.where(flat >= i * ROWS, PAD - ROWS, 0)
     mirror_own[...] = jnp.full((8, COLS), -1.0, F32)
     mirror_own[0:1, :ROWS] = row.astype(F32)
     pl.semaphore_wait(barrier, len(peers))
@@ -417,7 +418,7 @@
         ),
     )(
         amplitudes, ladder_ints, tile_map, hole_ints, occ_energy, pair_list.T,
-        mirror_row.reshape(1, -1),
+        mirror_row,
     )
     return out[:ROWS]
 

time: 90.7 us -> 89.4 us (0.986)
  local copies, waits for them, and re-layouts: 3.05 us -> 1.8 us
    reshape x1 -> x0, local copies, waits for them, and re-layouts: 1.24 us -> none  [shards(): mirror_row.reshape(1, -1)]
where the time goes in v1:
time: 89.4 us; the launch traced here: 89.3 us
  Pallas kernels  87.5 us (98%)
  local copies, waits for them, and re-layouts  1.8 us (2%)
    pallas_call x1, Pallas kernels, shards(): pl.pallas_call(kernel, name='ladder', out_shape=jax.ShapeDtypeStruct((PAD...  87.5 us
    unnamed x1, local copies, waits for them, and re-layouts  1.8 us

profile of v1, /device:TPU:11, one launch (start us, length us, event | category | flops | bytes accessed | tf_op | source)
XLA Modules:
  0.0 89.3 jit_solution(7443198642746290614)
XLA Ops:
  0.0 87.5 %ladder.1 = f32[288,384]{1,0:T(8,128)} custom-call(bf16[282,384]{1,0:T(8,128)(2,1)} %t_ref.1, bf16[384,1536]{1,0:T(8,128)(2,1)} %v_ref.1, s32[96,96]{1,0:T(8,128)} %tiles_ref.1, bf16[282,2256]{1,0:T(8,128)(2,1)} %w_ref.1, f32[48]{0:T(128)} %energy_ref.1, s32[2,282]{1,0:T(2,128)} %bitcast.3, s32[282]{0:T(512)} %mirror_ref.1), custom_call_target="tpu_custom_call" | custom-call | flops 10871635968 | bytes 6291456 | tf_op jit(solution)/shard_map/ladder/pallas_call | solution.py:379
  87.5 1.8 %copy.9 = f32[282,384]{1,0:T(8,128)} copy(f32[282,384]{1,0:T(8,128)} %bitcast.2) | data formatting | bytes 866304
